TPU v7x, 128 devices: a whole 4x4x4 slice. The times are simulated.
128 devices in a mesh: seq: 16 (over y_hi, z, core), enc: 8 (over x, y_lo).
Axes of the slice: x: 4, y: 4 (y_hi: 2, y_lo: 2; y = y_hi * 2 + y_lo), z: 4, core: 2. Of those that a mesh axis runs over, the one named last changes fastest.
Arguments:
- queries: bfloat16 [24576, 2048], P(('seq', 'enc')), may hold values from -10.2 to 10.2
- cond: bfloat16 [24576, 1024], P(('seq', 'enc')), may hold values from -10.2 to 10.2
- database: bfloat16 [256, 128, 1024], P('enc'), may hold values from -6 to 6
- neighbour_ids: int32 [384, 2], P(('seq', 'enc')), may hold values from 0 to 31
- owner_map: int32 [384, 2], P(('seq', 'enc')), may hold values from 0 to 7, as said below
- norm_gain: float32 [1024], replicated, may hold values from 0.1 to 1.9
- w_query_enc: bfloat16 [1024, 512], replicated, may hold values from -0.1875 to 0.1875
- w_out_enc: bfloat16 [512, 1024], replicated, may hold values from -0.25 to 0.25
- w_key_dec: bfloat16 [1024, 2048], replicated, may hold values from -0.1875 to 0.1875
- w_value_dec: bfloat16 [1024, 2048], replicated, may hold values from -0.1875 to 0.1875
- cotangent: bfloat16 [24576, 2048], P(('seq', 'enc')), may hold values from -6 to 6
Outputs:
- attended: bfloat16 [24576, 2048], P(('seq', 'enc'))
- grad_queries: bfloat16 [24576, 2048], P(('seq', 'enc'))
- grad_cond: bfloat16 [24576, 1024], P(('seq', 'enc'))
- grad_query_enc: float32 [1024, 512], P(('seq', 'enc'))
- grad_out_enc: float32 [512, 1024], P(('seq', 'enc'))
- grad_key_dec: float32 [1024, 2048], P(('seq', 'enc'))
- grad_value_dec: float32 [1024, 2048], P(('seq', 'enc'))
Inputs may be any that keep to these rules, and one draw needn't show every extreme that they name: `owner_map`: of the 6 neighbours of one device's spans at most 1 have the same owner; in every group of 8 devices along enc one owner gets exactly 1 from every device of the group.
All inputs are finite; a program needn't handle non-finite values.
Results may differ from a plain program's by a relative error of at most 0.018.
Values may be sent and summed in bfloat16 or wider, within the bound.
A program may use at most 192 MiB of HBM per device.

v0:
```python
import functools

import jax
import jax.numpy as jnp
from jax import lax
from jax.experimental import pallas as pl
from jax.experimental.pallas import tpu as pltpu
from jax.sharding import PartitionSpec as P

EPS = 1e-06
MESH = pl.DeviceIdType.MESH

F32, BF16 = jnp.float32, jnp.bfloat16
AXES = ("x", "y", "z")
TILES = 9
WHOLE_SLOTS = (
    (2, 3, 4, 5, 6, 7, 8, 9, 14),
    (6, 7, 8, 10, 11, 13, 15, 16, 18),
    (8, 9, 11, 13, 14, 16, 17, 18, 20),
    (10, 12, 14, 16, 17, 18, 19, 21, 22),
)
HALF_SLOTS = ((15, 16), (17, 18), (19, 20), (21, 22))
STEPS = 23
FIRST_AXES = (2, 0, 1, 2, 0, 2, 1, 2, 0)
HALF_SLOTS = ((15, 16), (17, 18), (19, 20), (21, 22))
SERVERS = ((0, 0), (0, 1), (1, 0), (1, -1), (2, 0), (2, 1), (3, 0), (3, -1))


def place():
    s, e = lax.axis_index("seq"), lax.axis_index("enc")
    return dict(core=s % 2, z=(s // 2) % 4, y=(s // 8) * 2 + e % 2, x=e // 2)


def device_of(at):
    y = at["y"]
    return ((y // 2) * 8 + at["z"] * 2 + at["core"], at["x"] * 2 + y % 2)


def moved(at, **steps):
    there = dict(at)
    for axis, step in steps.items():
        there[axis] = (at[axis] + step) % (2 if axis == "core" else 4)
    return there


def along(steps):
    p = (lax.axis_index("seq") * 8 + lax.axis_index("enc") + steps) % 128
    return (p // 8, p % 8)


def pick(index, values):
    if isinstance(index, int):
        return values[index]
    return jnp.where(index == 0, values[0], jnp.where(index == 1, values[1], values[2]))


def rows_of(axis, v):
    return ((0, 2 * v), (v // 2 * 4, v % 2), (v, 0))[axis]


def pick_pair(index, pairs):
    return tuple(pick(index, [pair[i] for pair in pairs]) for i in (0, 1))


class Map:
    def __init__(self):
        at = self.at = place()
        self.core = at["core"]
        self.other_core = device_of(moved(at, core=1))
        self.devices = [[device_of(moved(at, **{a: r})) for a in AXES] for r in range(4)]
        self.values = [[(at[a] + r) % 4 for a in AXES] for r in range(4)]
        self.places = [[rows_of(i, each[i]) for i in range(3)] for each in self.values]
        self.before, self.after = along(-1), along(1)


def remote(src, dst, send, recv, device):
    return pltpu.make_async_remote_copy(
        src_ref=src, dst_ref=dst, send_sem=send, recv_sem=recv, device_id=device, device_id_type=MESH
    )


def dot(a, b):
    return jnp.dot(a, b, preferred_element_type=F32)


def dot_nt(a, b):
    return lax.dot_general(a, b, (((1,), (1,)), ((), ())), preferred_element_type=F32)


def dot_tn(a, b):
    return lax.dot_general(a, b, (((0,), (0,)), ((), ())), preferred_element_type=F32)


class Tile:
    def __init__(self, map, t, turn, grads, came, sends, gets, kept, ssem, rsem, put):
        self.map, self.t, self.grads, self.came = map, t, grads, came
        self.sends, self.gets, self.kept = sends, gets, kept
        self.ssem, self.rsem, self.put = ssem, rsem, put
        if isinstance(turn, int):
            self.axes = [(turn + i) % 3 for i in range(3)]
        else:
            self.axes = [turn, jnp.where(turn == 2, 0, turn + 1), jnp.where(turn == 0, 2, turn - 1)]

    def value(self, level, r):
        return pick(self.axes[level], self.map.values[r])

    def copy(self, level, r=1):
        if level == 0:
            device, src, dst, sem = self.map.other_core, self.outgoing(), self.came, 0
        else:
            device = pick_pair(self.axes[level - 1], self.map.devices[r])
            src, dst, sem = self.sends[level - 1].at[r - 1], self.gets[level - 1].at[r - 1], 3 * level - 3 + r
        return remote(src, dst, self.ssem.at[self.t, sem], self.rsem.at[self.t, sem], device)

    def start(self):
        self.copy(0).start()

    def take(self, level):
        if level == 0:
            self.copy(0).wait_recv()
        else:
            for r in (1, 2, 3):
                self.copy(level, r).wait_recv()
        (self.take_core, self.take_first, self.take_second, self.take_third)[level]()

    def take_core(self):
        each = [
            [pick_pair(self.axes[level], [rows_of(a, v) for a in range(3)]) for v in range(4)] for level in (1, 2)
        ]
        rest = [tuple(a + b for a, b in zip(each[0][i // 4], each[1][i % 4])) for i in range(16)]
        for r in (2, 1, 3, 0):
            high, low = pick_pair(self.axes[0], self.map.places[r])
            for i in range(16):
                value = self.pair(high + rest[i][0], low + rest[i][1])
                if r:
                    self.sends[0][r - 1, i] = self.lower(value)
                else:
                    self.kept[0][i] = value
            if r:
                self.copy(1, r).start()
        self.copy(0).wait_send()

    def take_first(self):
        for r in (2, 1, 3, 0):
            first = self.value(1, r) * 4
            for i in range(4):
                c = first + i
                got = [self.higher(self.gets[0][q, c]) for q in range(3)]
                value = self.kept[0][c] + got[0] + got[1] + got[2]
                if r:
                    self.sends[1][r - 1, i] = value.astype(self.sends[1].dtype)
                else:
                    self.kept[1][i] = value
            if r:
                self.copy(2, r).start()

    def take_second(self):
        for r in (2, 1, 3, 0):
            c = self.value(2, r)
            got = [self.gets[1][q, c].astype(F32) for q in range(3)]
            value = self.kept[1][c] + got[0] + got[1] + got[2]
            if r:
                self.sends[2][r - 1, 0] = value.astype(self.sends[2].dtype)
                self.copy(3, r).start()
            else:
                self.kept[2][0] = value

    def take_third(self):
        got = [self.gets[2][q, 0].astype(F32) for q in range(3)]
        self.put(self.kept[2][0] + got[0] + got[1] + got[2])
        for level in (1, 2, 3):
            for r in (1, 2, 3):
                self.copy(level, r).wait_send()


class PairTile(Tile):
    def outgoing(self):
        return self.grads.at[:, :, 1 - self.map.core]

    def pair(self, high, low):
        core = self.map.core
        parts = [self.grads[i, high, core, low] + self.came[i, high, low] for i in (0, 1)]
        return jnp.concatenate(parts, axis=0)

    def lower(self, value):
        return value.astype(BF16)

    def higher(self, value):
        return value.astype(F32)


class HalfTile(Tile):
    def outgoing(self):
        return self.grads.at[:, 1 - self.map.core]

    def pair(self, high, low):
        return self.grads[high, self.map.core, low] + self.came[high, low]

    def lower(self, value):
        return jnp.concatenate([value[:, :128], value[:, 128:]], axis=0).astype(BF16)

    def higher(self, value):
        wide = value.astype(F32)
        return jnp.concatenate([wide[:8], wide[8:]], axis=1)


def by_head(x, reduce, neutral):
    low = lax.broadcasted_iota(jnp.int32, (x.shape[0], 128), 1) < 64
    parts = []
    for t in range(x.shape[1] // 128):
        one = x[:, t * 128 : t * 128 + 128]
        left = reduce(jnp.where(low, one, neutral), axis=-1, keepdims=True)
        right = reduce(jnp.where(low, neutral, one), axis=-1, keepdims=True)
        parts.append(jnp.where(low, left, right))
    return jnp.concatenate(parts, axis=1)


def head_blocks(x):
    wide = x.astype(F32)
    head = lax.broadcasted_iota(jnp.int32, x.shape, 1) // 64
    return jnp.concatenate([jnp.where(head == h, wide, 0.0) for h in range(4)], axis=0).astype(BF16)


def head_diagonal(x):
    head = lax.broadcasted_iota(jnp.int32, (64, 256), 1) // 64
    return sum(jnp.where(head == h, x[h * 64 : h * 64 + 64], 0.0) for h in range(4))


def two_heads(x):
    none = jnp.zeros((x.shape[0], 128), x.dtype)
    return jnp.concatenate(
        [jnp.concatenate([x[:, :128], none], axis=1), jnp.concatenate([none, x[:, 128:]], axis=1)], axis=0
    )


def own_heads(x):
    return jnp.concatenate([x[:64, :128], x[64:, 128:]], axis=1)


def main_kernel(
    ids, owners, database, cond_in, gain, wq_in, wo_in, wk_in, wv_in, q_in, g_in,
    att, dq_out, dcond, gq_out, go_out, gk_out, gv_out,
    pool, cond, wq, wo, wk, wv, q_ref, g_ref,
    asked, asks, blocks_out, upper_rows, lower_rows, later,
    normed, query, probs, mixed, src, kv, dmix, last, first,
    grads, came, send1, get1, send2, get2, send3, get3, kept1, kept2, kept3,
    hcame, hsend1, hget1, hsend2, hget2, hsend3, hget3, hkept1, hkept2, hkept3,
    load_sem, ask_s, ask_r, block_s, block_r, ahead_s, ahead_r, shift_s, shift_r, ssem, rsem,
):
    map = Map()
    at = map.at
    me = lax.axis_index("seq") * 8 + lax.axis_index("enc")
    loads = [
        pltpu.make_async_copy(a, b, load_sem.at[i])
        for i, (a, b) in enumerate(
            (
                (database, pool), (cond_in, cond), (wq_in, wq), (wo_in, wo),
                (wk_in, wk), (wv_in, wv), (q_in, q_ref), (g_in, g_ref),
            )
        )
    ]
    loads[0].start()

    barrier = pltpu.get_barrier_semaphore()
    steps = {(dx * s % 4, dy * s % 4) for dx, dy in SERVERS for s in (1, -1)} | {(0, 2)}
    steps = sorted(steps - {(0, 0)})
    peers = [device_of(moved(at, x=dx, y=dy)) for dx, dy in steps]
    peers += [device_of(moved(at, core=1))] + [device_of(moved(at, z=r)) for r in (1, 2, 3)]
    peers += [map.before, map.after]
    for peer in peers:
        pl.semaphore_signal(barrier, inc=1, device_id=peer, device_id_type=MESH)
    pl.semaphore_wait(barrier, len(peers))

    server = [((at["x"] + dx) % 4) * 2 + (at["y"] + dy) % 2 for dx, dy in SERVERS]

    def row_at(r):
        each = [(owners[j, s], ids[j, s]) for s in range(3) for j in range(2)]
        return sum(jnp.where(owner == server[r], row, 0) for owner, row in each)

    asking, answers = [], []
    for r in (5, 7, 3, 4, 2, 6, 1):
        dx, dy = SERVERS[r]
        asks[r] = jnp.full((8, 128), row_at(r), jnp.int32)
        copy = remote(
            asks.at[r], asked.at[r], ask_s.at[r], ask_r.at[r], device_of(moved(at, x=dx, y=dy))
        )
        copy.start()
        asking.append((r, copy))
    for copy in loads[1:]:
        copy.start()
    loads[0].wait()
    blocks = (upper_rows, lower_rows)
    for h in range(2):
        part = pl.ds(h * 64, 64)
        for r, copy in asking:
            dx, dy = SERVERS[r]
            if h == 0:
                copy.wait_recv()
                blocks_out[r] = pool[jnp.max(asked[r])]
            answer = remote(
                blocks_out.at[r, part], blocks[h].at[r], block_s.at[h, r], block_r.at[h, r],
                device_of(moved(at, x=-dx, y=-dy)),
            )
            answer.start()
            answers.append(answer)
    own = pool[row_at(0)]
    for h in range(2):
        blocks[h][0] = own[h * 64 : h * 64 + 64]
    for r, copy in asking:
        copy.wait_send()
    for copy in loads[1:4]:
        copy.wait()
    slots = [
        [sum(jnp.where(owners[j, s] == server[r], r, 0) for r in range(1, 8)) for j in range(2)] for s in range(3)
    ]

    def encode(h):
        low = h * 384
        both = slice(low, low + 384)
        for s in range(3):
            for j in range(2):
                at_rows = slice(low + s * 128 + j * 64, low + s * 128 + j * 64 + 64)
                raw = blocks[h][slots[s][j]].astype(F32)
                inverse = lax.rsqrt(jnp.mean(raw * raw, axis=-1, keepdims=True) + EPS)
                normed[at_rows, :] = (raw * inverse * gain[...]).astype(BF16)
        query[both, :] = dot(normed[both, :], wq[...]).astype(BF16)
        pieces = [(s, slice(c * 256, c * 256 + 256)) for s in range(3) for c in range(2)]
        here = [slice(low + s * 128, low + s * 128 + 128) for s in range(3)]
        span = [slice(s * 64, s * 64 + 64) for s in range(3)]
        k4 = [head_blocks(cond[span[s], c]) for s, c in pieces]
        v4 = [head_blocks(cond[span[s], c.start + 512 : c.stop + 512]) for s, c in pieces]
        scores = [dot_nt(query[here[s], c], k) * 0.125 for (s, c), k in zip(pieces, k4)]
        e = [jnp.exp(x - by_head(x, jnp.max, -jnp.inf)) for x in scores]
        p = [x / by_head(x, jnp.sum, 0.0) for x in e]
        for (s, c), x, v in zip(pieces, p, v4):
            probs[here[s], c] = x
            mixed[here[s], c] = dot(x.astype(BF16), v).astype(BF16)
        out = dot(mixed[both, :], wo[...])
        for s in range(3):
            for j in range(2):
                i = s * 128 + j * 64
                raw = blocks[h][slots[s][j]].astype(F32)
                src[low + i : low + i + 64, :] = (raw + out[i : i + 64]).astype(BF16)

    for answer in answers[:7]:
        answer.wait_recv()
    encode(0)
    for answer in answers[7:]:
        answer.wait_recv()

    def ahead(t):
        cols = pl.ds(pl.multiple_of(t * 256, 256), 256)
        return [
            remote(
                ref.at[pl.ds(0, 64), cols], later.at[i, :, cols], ahead_s.at[i, t], ahead_r.at[i, t], map.before
            )
            for i, ref in enumerate((q_in, g_in))
        ]

    def send_ahead(t, _):
        for copy in ahead(t):
            copy.start()
        return 0

    lax.fori_loop(0, 8, send_ahead, 0)
    encode(1)
    for copy in loads[4:]:
        copy.wait()
    for answer in answers:
        answer.wait_send()
    followed = jnp.where(me == 127, 0.0, 1.0).astype(BF16)

    def whole_tile(t):
        def put(total):
            def sheets():
                cols = pl.ds(pl.multiple_of(t * 256, 256), 256)
                gk_out[:, cols] = total[:8]
                gv_out[:, cols] = total[8:]

            def outer():
                for j in range(4):
                    go_out[:, j * 256 : j * 256 + 256] = total[j * 4 : j * 4 + 4]

            pl.when(t < 8)(sheets)
            pl.when(t == 8)(outer)

        turn = sum(jnp.where(t == i, a, 0) for i, a in enumerate(FIRST_AXES) if a)
        return PairTile(
            map, t, turn, grads.at[t % 3], came.at[t % 4],
            (send1.at[t], send2.at[t], send3.at[t]), (get1.at[t], get2.at[t], get3.at[t]),
            (kept1.at[t], kept2.at[t], kept3.at[t]), ssem, rsem, put,
        )

    def half_tile(i):
        def put(total):
            gq_out[:, pl.ds(pl.multiple_of(i * 256, 256), 256)] = total

        return HalfTile(
            map, TILES + i, 1 + i, grads.at[0, i], hcame.at[i],
            (hsend1.at[i], hsend2.at[i], hsend3.at[i]), (hget1.at[i], hget2.at[i], hget3.at[i]),
            (hkept1.at[i], hkept2.at[i], hkept3.at[i]), ssem, rsem, put,
        )

    scale = 128 ** (-0.5)

    def onward(t):
        cols = pl.ds(pl.multiple_of(t * 256, 256), 256)
        return [
            remote(last.at[i, :, cols], first.at[i, :, cols], shift_s.at[i, t], shift_r.at[i, t], map.after)
            for i in range(2)
        ]

    def of_span(ref, s, cols):
        return jnp.concatenate([ref[h * 384 + s * 128 : h * 384 + s * 128 + 128, cols] for h in range(2)], axis=0)

    def half_rows(t):
        return t // 4 * 6, pl.ds(pl.multiple_of(t % 4 * 256, 256), 256)

    def decode(t):
        cols = pl.ds(pl.multiple_of(t * 256, 256), 256)
        base, pool_cols = half_rows(t)
        for copy in ahead(t):
            copy.wait()
        kv[0] = dot(src[...], wk[:, cols]).astype(BF16)
        kv[1] = dot(src[...], wv[:, cols]).astype(BF16)
        k, v = ([of_span(kv.at[i], s, slice(None)) for s in range(3)] for i in range(2))
        afters = [slice(s * 64 + 64, s * 64 + 128) for s in range(3)]
        q2 = [two_heads(q_ref[a, cols]) for a in afters[:2]] + [two_heads(later[0, :, cols] * followed)]
        g2 = [two_heads(g_ref[a, cols]) for a in afters[:2]] + [two_heads(later[1, :, cols] * followed)]
        scores = [dot_nt(q2[s], k[s]) * scale for s in range(3)]
        dw = [dot_nt(g2[s], v[s]) for s in range(3)]
        e = [jnp.exp(x - jnp.max(x, axis=-1, keepdims=True)) for x in scores]
        p = [x / jnp.sum(x, axis=-1, keepdims=True) for x in e]
        w = [x.astype(BF16) for x in p]
        o = [own_heads(dot(w[s], v[s])).astype(BF16) for s in range(3)]
        dv = [dot_tn(w[s], g2[s]).astype(BF16) for s in range(3)]
        ds = [
            (p[s] * (dw[s] - jnp.sum(dw[s] * p[s], axis=-1, keepdims=True)) * scale).astype(BF16) for s in range(3)
        ]
        dq = [own_heads(dot(ds[s], k[s])).astype(BF16) for s in range(3)]
        dk = [dot_tn(ds[s], q2[s]).astype(BF16) for s in range(3)]
        for s in range(3):
            if s < 2:
                att[afters[s], cols] = o[s]
                dq_out[afters[s], cols] = dq[s]
            else:
                last[0, :, cols] = o[s]
                last[1, :, cols] = dq[s]
            for h in range(2):
                pool[base + h * 3 + s, :, pool_cols] = dk[s][h * 128 : h * 128 + 128]
                pool[base + h * 3 + s + 12, :, pool_cols] = dv[s][h * 128 : h * 128 + 128]
        for i in range(2):
            sheet = dot_tn(src[...], pool[pl.ds(base + 12 * i, 6), :, pool_cols].reshape(768, 256))
            grads[t % 3, i] = sheet.reshape(8, 2, 8, 8, 256)
        for copy in onward(t):
            copy.start()

    def sources_back(i):
        cols = pl.ds(pl.multiple_of(i * 256, 256), 256)
        total = sum(
            dot_nt(pool[j * 6 : j * 6 + 6].reshape(768, 1024), w[cols, j % 2 * 1024 : j % 2 * 1024 + 1024])
            for j, w in enumerate((wk, wk, wv, wv))
        )
        pool[24:30, :, cols] = total.astype(BF16).reshape(6, 128, 256)

    def outer_out():
        for i in range(2):
            for j in range(2):
                cols = slice(i * 512 + j * 256, i * 512 + j * 256 + 256)
                sheet = dot_tn(mixed[...], pool[24:30, :, cols].reshape(768, 256))
                grads[1, j, 0:4] = sheet.reshape(4, 2, 8, 8, 256)

            def stack(g, _, i=i):
                for q in range(8):
                    left, right = (grads[1, j, g // 2, g % 2, q] for j in (0, 1))
                    for upper in range(2):
                        rows = slice(upper * 4, upper * 4 + 4)
                        p = 2 * q + upper
                        grads[2, i, g, p // 8, p % 8] = jnp.concatenate([left[rows], right[rows]], axis=0)
                return 0

            lax.fori_loop(0, 8, stack, 0)
        whole_tile(8).start()

    def mixed_back():
        dmix[...] = dot_nt(pool[24:30].reshape(768, 1024), wo[...]).astype(BF16)

    def query_back(half):
        cols = pl.ds(pl.multiple_of(half * 256, 256), 256)
        vcols = pl.ds(pl.multiple_of(half * 256 + 512, 256), 256)
        spans = [slice(s * 64, s * 64 + 64) for s in range(3)]
        k4 = [head_blocks(cond[span, cols]) for span in spans]
        v4 = [head_blocks(cond[span, vcols]) for span in spans]
        dw = [dot_nt(of_span(dmix, s, cols), v4[s]) for s in range(3)]
        p = [of_span(probs, s, cols) for s in range(3)]
        sums = [by_head(dw[s] * p[s], jnp.sum, 0.0) for s in range(3)]
        ds = [(p[s] * (dw[s] - sums[s]) * 0.125).astype(BF16) for s in range(3)]
        for s in range(3):
            dquery = dot(ds[s], k4[s]).astype(BF16)
            for h in range(2):
                rows, part = pl.ds(h * 384 + s * 128, 128), slice(h * 128, h * 128 + 128)
                mixed[rows, cols] = ds[s][part]
                kv[half, rows, :] = dquery[part]
        grads[0, half] = dot_tn(normed[...], kv[half]).reshape(8, 2, 8, 8, 256)
        half_tile(half).start()

    def cond_back():
        def some(i, _):
            s, half = i // 2, i % 2
            span = pl.ds(pl.multiple_of(s * 64, 64), 64)
            cols = pl.ds(pl.multiple_of(half * 256, 256), 256)
            vcols = pl.ds(pl.multiple_of(half * 256 + 512, 256), 256)

            def both(ref):
                parts = [ref[pl.ds(pl.multiple_of(h * 384 + s * 128, 128), 128), cols] for h in range(2)]
                return jnp.concatenate(parts, axis=0)

            w = both(probs).astype(BF16)
            dcond[span, vcols] = head_diagonal(dot_tn(w, both(dmix))).astype(BF16)
            dcond[span, cols] = head_diagonal(dot_tn(both(mixed), both(query))).astype(BF16)
            return 0

        lax.fori_loop(0, 6, some, 0)

    def tile_at(slot, slots):
        return sum(jnp.where(slot == at_slot, t + 1, 0) for t, at_slot in enumerate(slots)) - 1

    def step(slot, _):
        pl.when(slot < 8)(lambda: decode(slot))
        pl.when((slot >= 8) & (slot < 12))(lambda: sources_back(slot - 8))
        pl.when(slot == 12)(outer_out)
        pl.when(slot == 13)(mixed_back)
        pl.when((slot == 14) | (slot == 15))(lambda: query_back(slot - 14))
        pl.when(slot == 16)(cond_back)
        def take_halves(levels):
            for level in levels:
                i = tile_at(slot, HALF_SLOTS[level])
                pl.when(i >= 0)(lambda i=i, level=level: half_tile(i).take(level))

        take_halves((3, 2, 1))
        for level in (3, 2, 1, 0):
            t = tile_at(slot, WHOLE_SLOTS[level])
            pl.when(t >= 0)(lambda t=t, level=level: whole_tile(t).take(level))
        take_halves((0,))
        pl.when(slot < 8)(lambda: whole_tile(slot).start())
        return 0

    lax.fori_loop(0, STEPS, step, 0)

    def arrive(t, _):
        for copy in onward(t):
            copy.wait()
        return 0

    lax.fori_loop(0, 8, arrive, 0)
    followed_by = jnp.where(me == 0, 0.0, 1.0).astype(BF16)
    att[:64, :] = first[0] * followed_by
    dq_out[:64, :] = first[1] * followed_by


def fused(ids, owners, database, cond, gain, wq, wo, wk, wv, queries, grads):
    vmem, smem = pl.BlockSpec(memory_space=pltpu.VMEM), pl.BlockSpec(memory_space=pltpu.SMEM)
    hbm = pl.BlockSpec(memory_space=pl.ANY)
    shape, dma = jax.ShapeDtypeStruct, pltpu.SemaphoreType.DMA
    half = lambda *dims: pltpu.VMEM(dims, BF16)
    full = lambda *dims: pltpu.VMEM(dims, F32)
    outs = pl.pallas_call(
        main_kernel,
        out_shape=(
            shape((192, 2048), BF16),
            shape((192, 2048), BF16),
            shape((192, 1024), BF16),
            shape((8, 512), F32),
            shape((4, 1024), F32),
            shape((8, 2048), F32),
            shape((8, 2048), F32),
        ),
        in_specs=[smem, smem, hbm, hbm, vmem] + [hbm] * 6,
        out_specs=(vmem,) * 7,
        scratch_shapes=[
            half(32, 128, 1024), half(192, 1024), half(1024, 512), half(512, 1024),
            half(1024, 2048), half(1024, 2048), half(192, 2048), half(192, 2048),
            pltpu.VMEM((8, 8, 128), jnp.int32), pltpu.VMEM((8, 8, 128), jnp.int32),
            half(8, 128, 1024), half(8, 64, 1024), half(8, 64, 1024), half(2, 64, 2048),
            half(768, 1024), half(768, 512), full(768, 512), half(768, 512), half(768, 1024),
            half(2, 768, 256), half(768, 512),
            half(2, 64, 2048), half(2, 64, 2048),
            full(3, 2, 8, 2, 8, 8, 256), full(4, 2, 8, 8, 8, 256),
            half(TILES, 3, 16, 16, 256), half(TILES, 3, 16, 16, 256),
            half(TILES, 3, 4, 16, 256), half(TILES, 3, 4, 16, 256),
            half(TILES, 3, 1, 16, 256), half(TILES, 3, 1, 16, 256),
            full(TILES, 16, 16, 256), full(TILES, 4, 16, 256), full(TILES, 1, 16, 256),
            full(2, 8, 8, 8, 256), half(2, 3, 16, 16, 128), half(2, 3, 16, 16, 128),
            full(2, 3, 4, 8, 256), full(2, 3, 4, 8, 256), full(2, 3, 1, 8, 256), full(2, 3, 1, 8, 256),
            full(2, 16, 8, 256), full(2, 4, 8, 256), full(2, 1, 8, 256),
            dma((8,)), dma((8,)), dma((8,)), dma((2, 8)), dma((2, 8)), dma((2, 8)), dma((2, 8)), dma((2, 8)), dma((2, 8)),
            dma((TILES + 2, 10)), dma((TILES + 2, 10)),
        ],
        compiler_params=pltpu.CompilerParams(
            collective_id=0, has_side_effects=True, vmem_limit_bytes=63 * 1024 * 1024
        ),
    )(ids, owners, database, cond, gain, wq, wo, wk, wv, queries, grads)

    def leave(*refs):
        n, sem = len(outs), refs[-1]
        copies = [pltpu.make_async_copy(refs[i], refs[n + i], sem.at[i]) for i in range(n)]
        for copy in copies:
            copy.start()
        for copy in copies:
            copy.wait()

    return pl.pallas_call(
        leave,
        out_shape=tuple(shape(o.shape, o.dtype) for o in outs),
        in_specs=[hbm] * len(outs),
        out_specs=(vmem,) * len(outs),
        scratch_shapes=[dma((len(outs),))],
    )(*outs)


def body(
    queries,
    cond,
    database,
    neighbour_ids,
    owner_map,
    norm_gain,
    w_query_enc,
    w_out_enc,
    w_key_dec,
    w_value_dec,
    cotangent,
):
    return fused(
        neighbour_ids.T,
        owner_map.T,
        database,
        cond,
        norm_gain.reshape(1, -1),
        w_query_enc,
        w_out_enc,
        w_key_dec,
        w_value_dec,
        queries,
        cotangent,
    )


def solution(mesh):
    tokens = P(("seq", "enc"), None)
    return jax.shard_map(
        body,
        mesh=mesh,
        in_specs=(tokens, tokens, P("enc", None, None), tokens, tokens, P(), P(), P(), P(), P(), tokens),
        out_specs=(tokens,) * 7,
        check_vma=False,
    )
```

profile of v0, /device:TPU:0, one launch (start us, length us, event | category | flops | bytes accessed | tf_op | source)
XLA Modules:
  0.0 106.6 jit_solution(11455786645265022641)
XLA Ops:
  0.6 102.9 %shard_map.162 = (bf16[192,2048]{1,0:T(8,128)(2,1)}, bf16[192,2048]{1,0:T(8,128)(2,1)}, bf16[192,1024]{1,0:T(8,128)(2,1)}, f32[8,512]{1,0:T(8,128)}, f32[4,1024]...) custom-call(s32[2,3]{1,0:T(2,128)} %bitcast.4, s32[2,3]{1,0:T(2,128)} %bitcast.5, bf16[32,128,1024]{2,1,0:T(8,128)(2,1)} %database.1, ...), custom_call_target="tpu_custom_call" | custom-call | tf_op jit(solution)/shard_map/pallas_call | solution.py:567
  103.5 2.9 %shard_map.163 = (bf16[192,2048]{1,0:T(8,128)(2,1)}, bf16[192,2048]{1,0:T(8,128)(2,1)}, bf16[192,1024]{1,0:T(8,128)(2,1)}, f32[8,512]{1,0:T(8,128)}, f32[4,1024]...) custom-call(bf16[192,2048]{1,0:T(8,128)(2,1)} %get-tuple-element.14.refs_0_, ...), custom_call_target="tpu_custom_call" | custom-call | tf_op jit(solution)/shard_map/pallas_call | solution.py:612
where the time goes:
time: 107 us
  Pallas kernels  106 us (99%)
    pallas_call x1, Pallas kernels, fused(): pl.pallas_call(main_kernel, out_shape=(shape((192, 2048), BF16), shape((1...  103 us
    pallas_call x1, Pallas kernels, fused(): pl.pallas_call(leave, out_shape=tuple((shape(o.shape, o.dtype) for o in o...  2.86 us

commit v1 on v0

--- a/solution.py
+++ b/solution.py
@@ -342,12 +342,6 @@
                 raw = blocks[h][slots[s][j]].astype(F32)
                 src[low + i : low + i + 64, :] = (raw + out[i : i + 64]).astype(BF16)
 
-    for answer in answers[:7]:
-        answer.wait_recv()
-    encode(0)
-    for answer in answers[7:]:
-        answer.wait_recv()
-
     def ahead(t):
         cols = pl.ds(pl.multiple_of(t * 256, 256), 256)
         return [
@@ -362,7 +356,17 @@
             copy.start()
         return 0
 
-    lax.fori_loop(0, 8, send_ahead, 0)
+    def send_all_ahead():
+        lax.fori_loop(0, 8, send_ahead, 0)
+
+    pl.when(at["y"] % 2 == 1)(send_all_ahead)
+    for answer in answers[:7]:
+        answer.wait_recv()
+    encode(0)
+    for answer in answers[7:]:
+        answer.wait_recv()
+
+    pl.when(at["y"] % 2 == 0)(send_all_ahead)
     encode(1)
     for copy in loads[4:]:
         copy.wait()

time: 107 us -> 106 us (level)
  no operation moved by 1% of the time
where the time goes in v1:
time: 106 us
  Pallas kernels  105 us (99%)
    pallas_call x1, Pallas kernels, fused(): pl.pallas_call(main_kernel, out_shape=(shape((192, 2048), BF16), shape((1...  102 us
    pallas_call x1, Pallas kernels, fused(): pl.pallas_call(leave, out_shape=tuple((shape(o.shape, o.dtype) for o in o...  2.86 us

profile of v1, /device:TPU:0, one launch (start us, length us, event | category | flops | bytes accessed | tf_op | source)
XLA Modules:
  0.0 105.8 jit_solution(3703453245044540287)
XLA Ops:
  0.6 102.2 %shard_map.162 = (bf16[192,2048]{1,0:T(8,128)(2,1)}, bf16[192,2048]{1,0:T(8,128)(2,1)}, bf16[192,1024]{1,0:T(8,128)(2,1)}, f32[8,512]{1,0:T(8,128)}, f32[4,1024]...) custom-call(s32[2,3]{1,0:T(2,128)} %bitcast.4, s32[2,3]{1,0:T(2,128)} %bitcast.5, bf16[32,128,1024]{2,1,0:T(8,128)(2,1)} %database.1, ...), custom_call_target="tpu_custom_call" | custom-call | tf_op jit(solution)/shard_map/pallas_call | solution.py:571
  102.8 2.9 %shard_map.163 = (bf16[192,2048]{1,0:T(8,128)(2,1)}, bf16[192,2048]{1,0:T(8,128)(2,1)}, bf16[192,1024]{1,0:T(8,128)(2,1)}, f32[8,512]{1,0:T(8,128)}, f32[4,1024]...) custom-call(bf16[192,2048]{1,0:T(8,128)(2,1)} %get-tuple-element.14.refs_0_, ...), custom_call_target="tpu_custom_call" | custom-call | tf_op jit(solution)/shard_map/pallas_call | solution.py:616
